TPU v7x, 512 devices: a whole 4x8x8 slice. The times are simulated.
512 devices in a mesh: horiz: 128 (over z, y, core), lev: 4 (over x).
Axes of the slice: x: 4, y: 8, z: 8, core: 2. Of those that a mesh axis runs over, the one named last changes fastest.
Arguments:
- jacobian: bfloat16 [8192, 2, 136, 200], P('horiz', None, 'lev'), may hold values from -0.375 to 0.375
- obs_tile: int32 [8192, 1], P('horiz'), may hold values from 0 to 127; in each aligned block of 64 rows (0 to 63, 64 to 127, ...) at most 2 rows name the same one
- obs_column: int32 [8192], P('horiz'), may hold values from 0 to 511
- obs_weight: float32 [8192], P('horiz'), may hold values from 0.25 to 4
- innovation: float32 [8192, 200], P('horiz'), may hold values from -12 to 12
- precision_off: float32 [200, 200], replicated, may hold values from -0.03 to 0.03
- vertical_factor: float32 [2, 136, 136], replicated, may hold values from -0.05 to 0.05
Outputs:
- increment: float32 [136, 2, 65536], P('lev', None, 'horiz')
- residual: float32 [136, 2, 65536], P('lev', None, 'horiz')
Inputs may be any that keep to these rules, and one draw needn't show every extreme that they name: `obs_tile`: among the 64 observations of one index of horiz, at most 2 fall in one tile, and some tile takes exactly 2.
All inputs are finite; a program needn't handle non-finite values.
Results may differ from a plain program's by a relative error of at most 0.008.
Values may be sent and summed in bfloat16 or wider, within the bound.
A program may use at most 128 MiB of HBM per device.

v0:
```python
import jax
import jax.numpy as jnp
from jax import lax
from jax.sharding import PartitionSpec as P

COLS = 512
ITERS = 2


def shards(jacobian, obs_tile, obs_column, obs_weight, innovation, precision_off, vertical_factor):
    highest = lax.Precision.HIGHEST
    tile_count = lax.axis_size("horiz")
    obs_count = jacobian.shape[0]
    band_size = jacobian.shape[2]
    channels = jacobian.shape[3]
    capacity = max(2, 2 * obs_count // tile_count)
    slot_count = tile_count * capacity
    target = obs_tile[:, 0]
    tile_onehot = (target[:, None] == jnp.arange(tile_count, dtype=jnp.int32)[None, :]).astype(
        jnp.int32
    )
    position = jnp.sum(tile_onehot * (jnp.cumsum(tile_onehot, axis=0) - 1), axis=1)
    slot_index = target * capacity + position
    precision_matrix = jnp.eye(channels, dtype=jnp.float32) + 0.5 * (
        precision_off + precision_off.T
    )
    levels = vertical_factor.shape[1]
    factor = jnp.eye(levels, dtype=jnp.float32)[None] + vertical_factor
    band_start = lax.axis_index("lev") * band_size
    forward_rows = lax.dynamic_slice_in_dim(factor, band_start, band_size, 1)
    forward_cols = lax.dynamic_slice_in_dim(factor, band_start, band_size, 2)
    adjoint_rows = jnp.swapaxes(forward_cols, 1, 2)
    slot_weight = jnp.zeros((slot_count,), jnp.float32).at[slot_index].set(obs_weight)
    slot_innovation = jnp.zeros((slot_count, channels), jnp.float32).at[slot_index].set(innovation)
    slot_column = jnp.zeros((slot_count,), jnp.int32).at[slot_index].set(obs_column)

    def vertical(column_field, rows_matrix):
        return jnp.einsum(
            "vij,jvc->ivc",
            rows_matrix,
            lax.all_gather(column_field, "lev", axis=0, tiled=True),
            precision=highest,
        )

    def global_sum(values):
        return lax.psum(values, ("horiz", "lev"))

    def weigh(values, weights):
        return weights[:, None] * jnp.dot(values, precision_matrix, precision=highest)

    jac_buffer = (
        jnp.zeros((slot_count, 2, band_size, channels), jnp.bfloat16).at[slot_index].set(jacobian)
    )
    received_jac = lax.all_to_all(jac_buffer, "horiz", split_axis=0, concat_axis=0, tiled=True)
    column_ids = lax.all_to_all(slot_column, "horiz", split_axis=0, concat_axis=0, tiled=True)
    column_onehot = (column_ids[:, None] == jnp.arange(COLS, dtype=jnp.int32)[None, :]).astype(
        jnp.float32
    )

    def to_columns(terms):
        return jnp.einsum("ivs,sc->ivc", terms, column_onehot, precision=highest)

    def grid_terms(weighted):
        return to_columns(
            jnp.einsum("svic,sc->ivs", received_jac, weighted, preferred_element_type=jnp.float32)
        )

    def return_weighted(arrived):
        return lax.all_to_all(
            weigh(arrived, slot_weight).astype(jnp.bfloat16),
            "horiz",
            split_axis=0,
            concat_axis=0,
            tiled=True,
        )

    start_terms = grid_terms(return_weighted(slot_innovation))
    rhs = vertical(start_terms, adjoint_rows)
    increment = jnp.zeros_like(rhs)
    residual = rhs
    direction = rhs
    norm_now = global_sum(jnp.sum(residual * residual))
    for iteration in range(ITERS):
        lifted = vertical(direction, forward_rows)
        sent = jnp.take(lifted, column_ids, axis=2).astype(jnp.bfloat16)
        images = lax.psum(
            jnp.einsum("svic,ivs->sc", received_jac, sent, preferred_element_type=jnp.float32),
            "lev",
        )
        observe_arrived = lax.all_to_all(images, "horiz", split_axis=0, concat_axis=0, tiled=True)
        image = direction + vertical(grid_terms(return_weighted(observe_arrived)), adjoint_rows)
        step_length = norm_now / global_sum(jnp.sum(direction * image))
        increment = increment + step_length * direction
        residual = residual - step_length * image
        norm_next = global_sum(jnp.sum(residual * residual))
        direction = residual + norm_next / norm_now * direction
        norm_now = norm_next
    return (increment, residual)


def solution(mesh):
    return jax.shard_map(
        shards,
        mesh=mesh,
        in_specs=(
            P("horiz", None, "lev", None),
            P("horiz", None),
            P("horiz"),
            P("horiz"),
            P("horiz", None),
            P(),
            P(),
        ),
        out_specs=(P("lev", None, "horiz"), P("lev", None, "horiz")),
        check_vma=False,
    )
```

profile of v0, /device:TPU:1, one launch (start us, length us, event | category | flops | bytes accessed | tf_op | source)
XLA Modules:
  0.0 962.4 jit_solution(3184242755278603639)
XLA Ops:
  11.3 18.4 %all-to-all-start.2 = ((s32[128,2,1]{1,2,0:T(1,128)}), s32[128,2,1]{1,2,0:T(1,128)S(1)}, u32[]{:S(2)}, u32[]{:S(2)}) async-start(s32[128,2,1]{1,2,0:T(1,128)} %bitcast.6), calls=%async_computation.2 | async-start | bytes 131072 | tf_op jit(solution)/shard_map/all_to_all | solution.py:55
  30.7 1.2 scatter_custom_fusion.1
  31.9 1.0 copy.20
  32.9 1.5 fusion.12
  35.3 5.9 all-to-all-done.2
  41.1 7.9 all-to-all-start
  49.0 5.8 broadcast_in_dim.19
  54.8 15.0 %scatter_fusion = bf16[256,2,34,200]{3,1,2,0:T(2,128)(2,1)} fusion(bf16[256,2,34,200]{3,1,2,0:T(2,128)(2,1)} %broadcast_in_dim.19, s32[64]{0:T(128)S(1)} %fusion.48, bf16[64,2,34,200]{3,1,2,0:T(2,128)(2,1)S(1)} %copy-done.1), kind=kCustom, calls=%fused_computation.4 | custom fusion | bytes 5222656 | tf_op jit(solution)/shard_map/scatter | solution.py:52
  69.8 14.3 %all-to-all-start.1 = ((bf16[256,2,34,200]{3,1,2,0:T(2,128)(2,1)}), bf16[256,2,34,200]{3,1,2,0:T(2,128)(2,1)}, u32[]{:S(2)}, u32[]{:S(2)}) async-start(bf16[256,2,34,200]{3,1,2,0:T(2,128)(2,1)} %scatter_fusion), calls=%async_computation.1 | async-start | bytes 17825792 | tf_op jit(solution)/shard_map/all_to_all | solution.py:54
  86.2 253.9 %all-to-all-done.1 = bf16[256,2,34,200]{3,1,2,0:T(2,128)(2,1)} async-done(((bf16[256,2,34,200]{3,1,2,0:T(2,128)(2,1)}), bf16[256,2,34,200]{3,1,2,0:T(2,128)(2,1)}, u32[]{:S(2)}, u32[]{:S(2)}) %all-to-all-start.1) | async-done | bytes 6963232 | tf_op jit(solution)/shard_map/all_to_all | solution.py:54
  340.1 9.3 fusion.8
  350.1 10.4 %all_gather.15 = f32[136,2,512]{2,1,0:T(2,128)S(1)} all-gather(f32[34,2,512]{2,1,0:T(2,128)S(1)} %copy.23), channel_id=1, replica_groups=mesh['horiz'=128,'lev'=4] {'lev'}, dimensions={0}, use_global_device_ids=true | all-gather | bytes 696320 | tf_op jit(solution)/shard_map/all_gather | solution.py:41
  361.1 11.3 %all_gather.16 = f32[136,2,512]{2,1,0:T(2,128)S(1)} all-gather(f32[34,2,512]{2,1,0:T(2,128)S(1)} %copy.26), channel_id=1, replica_groups=mesh['horiz'=128,'lev'=4] {'lev'}, dimensions={0}, use_global_device_ids=true | all-gather | bytes 696320 | tf_op jit(solution)/shard_map/all_gather | solution.py:41
  373.2 0.9 gather_fusion
  374.5 5.1 fusion.6
  380.6 71.7 %all-reduce.4.cloned.1.call-done = f32[128,2,200]{2,1,0:T(2,128)} async-done(((f32[128,2,200]{2,1,0:T(2,128)}), f32[128,2,200]{2,1,0:T(2,128)}) %all-reduce.4.cloned.1.call-update) | async-done | bytes 204816 | tf_op jit(solution)/shard_map/psum | solution.py:86
  452.3 31.7 %all_to_all.74 = f32[128,2,200]{2,1,0:T(2,128)S(1)} all-to-all(f32[128,2,200]{2,1,0:T(2,128)} %all-reduce.4.cloned.1.call-done), channel_id=1, replica_groups=mesh['horiz'=128,'lev'=4] {'horiz'}, dimensions={0} | all-to-all | bytes 409600 | tf_op jit(solution)/shard_map/all_to_all | solution.py:90
  484.9 17.9 %all_to_all.75 = bf16[128,2,200]{2,1,0:T(2,128)(2,1)S(1)} all-to-all(bf16[128,2,200]{2,1,0:T(2,128)(2,1)S(1)} %all_to_all.58), channel_id=1, replica_groups=mesh['horiz'=128,'lev'=4] {'horiz'}, dimensions={0} | all-to-all | bytes 204800 | tf_op jit(solution)/shard_map/all_to_all | solution.py:69
  503.0 9.3 fusion.4
  513.0 10.0 %all_gather.17 = f32[136,2,512]{2,1,0:T(2,128)S(1)} all-gather(f32[34,2,512]{2,1,0:T(2,128)S(1)} %copy.31), channel_id=1, replica_groups=mesh['horiz'=128,'lev'=4] {'lev'}, dimensions={0}, use_global_device_ids=true | all-gather | bytes 696320 | tf_op jit(solution)/shard_map/all_gather | solution.py:41
  522.9 1.1 multiply_reduce_fusion.2
  524.1 96.4 %all-reduce = (f32[]{:T(128)}, f32[]{:T(128)}) all-reduce(f32[]{:T(128)} %get-tuple-element.10, f32[]{:T(128)} %get-tuple-element.9), channel_id=1, replica_groups=mesh['horiz'=128,'lev'=4] {'horiz','lev'}, use_global_device_ids=true, to_apply=%region_7.8 | all-reduce | flops 2 | bytes 16 | tf_op jit(solution)/shard_map/psum | solution.py:46
  622.4 94.0 %psum.45 = f32[]{:T(128)} all-reduce(f32[]{:T(128)} %multiply_reduce_fusion.1), channel_id=1, replica_groups=mesh['horiz'=128,'lev'=4] {'horiz','lev'}, use_global_device_ids=true, to_apply=%region_12.14 | all-reduce | flops 1 | bytes 8 | tf_op jit(solution)/shard_map/psum | solution.py:46
  717.9 10.2 %all_gather.18 = f32[136,2,512]{2,1,0:T(2,128)S(1)} all-gather(f32[34,2,512]{2,1,0:T(2,128)S(1)} %copy.33), channel_id=1, replica_groups=mesh['horiz'=128,'lev'=4] {'lev'}, dimensions={0}, use_global_device_ids=true | all-gather | bytes 696320 | tf_op jit(solution)/shard_map/all_gather | solution.py:41
  730.2 5.1 fusion.2
  736.1 48.2 %all-reduce.6.cloned.1.call-done = f32[128,2,200]{2,1,0:T(2,128)} async-done(((f32[128,2,200]{2,1,0:T(2,128)}), f32[128,2,200]{2,1,0:T(2,128)}) %all-reduce.6.cloned.1.call-update) | async-done | bytes 204816 | tf_op jit(solution)/shard_map/psum | solution.py:86
  784.4 31.7 %all_to_all.76 = f32[128,2,200]{2,1,0:T(2,128)S(1)} all-to-all(f32[128,2,200]{2,1,0:T(2,128)} %all-reduce.6.cloned.1.call-done), channel_id=1, replica_groups=mesh['horiz'=128,'lev'=4] {'horiz'}, dimensions={0} | all-to-all | bytes 409600 | tf_op jit(solution)/shard_map/all_to_all | solution.py:90
  817.0 17.7 %all_to_all.77 = bf16[128,2,200]{2,1,0:T(2,128)(2,1)S(1)} all-to-all(bf16[128,2,200]{2,1,0:T(2,128)(2,1)S(1)} %all_to_all.64), channel_id=1, replica_groups=mesh['horiz'=128,'lev'=4] {'horiz'}, dimensions={0} | all-to-all | bytes 204800 | tf_op jit(solution)/shard_map/all_to_all | solution.py:69
  834.9 9.3 fusion
  844.8 10.0 %all_gather.19 = f32[136,2,512]{2,1,0:T(2,128)S(1)} all-gather(f32[34,2,512]{2,1,0:T(2,128)S(1)} %copy.38), channel_id=1, replica_groups=mesh['horiz'=128,'lev'=4] {'lev'}, dimensions={0}, use_global_device_ids=true | all-gather | bytes 696320 | tf_op jit(solution)/shard_map/all_gather | solution.py:41
  854.8 1.1 multiply_reduce_fusion
  855.9 96.3 %psum.47 = f32[]{:T(128)} all-reduce(f32[]{:T(128)} %get-tuple-element.16), channel_id=1, replica_groups=mesh['horiz'=128,'lev'=4] {'horiz','lev'}, use_global_device_ids=true, to_apply=%region_15.17 | all-reduce | flops 1 | bytes 8 | tf_op jit(solution)/shard_map/psum | solution.py:46
  (68 shorter events, 20.1 us)
Async XLA Ops:
  7.2 47.6 %copy-start.1 = (bf16[64,2,34,200]{3,1,2,0:T(2,128)(2,1)S(1)}, bf16[64,2,34,200]{3,1,2,0:T(2,128)(2,1)}, u32[]{:S(2)}) copy-start(bf16[64,2,34,200]{3,1,2,0:T(2,128)(2,1)} %param.9) | copy-start | bytes 5222404
  11.3 29.8 %all-to-all-start.2 = ((s32[128,2,1]{1,2,0:T(1,128)}), s32[128,2,1]{1,2,0:T(1,128)S(1)}, u32[]{:S(2)}, u32[]{:S(2)}) async-start(s32[128,2,1]{1,2,0:T(1,128)} %bitcast.6), calls=%async_computation.2 | async-start | bytes 131072 | tf_op jit(solution)/shard_map/all_to_all | solution.py:55
  41.1 28.6 %all-to-all-start = ((bf16[128,2,200]{2,1,0:T(2,128)(2,1)}), bf16[128,2,200]{2,1,0:T(2,128)(2,1)S(1)}, u32[]{:S(2)}, u32[]{:S(2)}) async-start(bf16[128,2,200]{2,1,0:T(2,128)(2,1)} %all_to_all.49), calls=%async_computation | async-start | bytes 262144 | tf_op jit(solution)/shard_map/all_to_all | solution.py:69
  69.8 14.5 %copy-start.2 = (f32[2,136,136]{2,1,0:T(8,128)S(1)}, f32[2,136,136]{2,1,0:T(8,128)}, u32[]{:S(2)}) copy-start(f32[2,136,136]{2,1,0:T(8,128)} %param.15) | copy-start | bytes 443908
  69.8 270.4 %all-to-all-start.1 = ((bf16[256,2,34,200]{3,1,2,0:T(2,128)(2,1)}), bf16[256,2,34,200]{3,1,2,0:T(2,128)(2,1)}, u32[]{:S(2)}, u32[]{:S(2)}) async-start(bf16[256,2,34,200]{3,1,2,0:T(2,128)(2,1)} %scatter_fusion), calls=%async_computation.1 | async-start | bytes 17825792 | tf_op jit(solution)/shard_map/all_to_all | solution.py:54
  84.1 368.2 %all-reduce.4.cloned.1.call-start = ((), (), s32[]{:S(2)}) async-start(), calls=%async_computation.7 | async-start | bytes 524288 | tf_op jit(solution)/shard_map/psum | solution.py:86
  374.5 109.7 %copy-start = (f32[200,200]{1,0:T(8,128)S(1)}, f32[200,200]{1,0:T(8,128)}, u32[]{:S(2)}) copy-start(f32[200,200]{1,0:T(8,128)} %param.14) | copy-start | bytes 480004
  380.5 403.8 %all-reduce.6.cloned.1.call-start = ((), (), s32[]{:S(2)}) async-start(), calls=%async_computation.8 | async-start | bytes 524288 | tf_op jit(solution)/shard_map/psum | solution.py:86
Sparse Core Ops, SparseCore 0:
  380.6 71.6 all-reduce.3
  736.3 48.0 all-reduce.5
where the time goes:
time: 970 us; the launch traced here: 962 us
  blocking collectives  437 us (45%)
  waiting for transfers between devices  380 us (39%)
  matrix products  45.8 us (5%)
  starting transfers between devices  40.8 us (4%)
  local copies, waits for them, and re-layouts  35 us (4%)
  between operations  18.8 us (2%)
    psum x3, blocking collectives, global_sum(): return lax.psum(values, ('horiz', 'lev'))  287 us
    all_to_all x1, waiting for transfers between devices, shards(): lax.all_to_all(jac_buffer, 'horiz', split_axis=0, concat_axis=0, tiled=True)  254 us
    psum x2, waiting for transfers between devices, shards(): lax.psum(jnp.einsum('svic,ivs->sc', received_jac, sent, preferred_element...  120 us
    all_to_all x2, blocking collectives, shards(): lax.all_to_all(images, 'horiz', split_axis=0, concat_axis=0, tiled=True)  63.3 us
    all_gather x5, blocking collectives, vertical(): lax.all_gather(column_field, 'lev', axis=0, tiled=True)  51.8 us
    all_to_all x2, blocking collectives, return_weighted(): lax.all_to_all(weigh(arrived, slot_weight).astype(jnp.bfloat16), 'horiz',...  35.6 us
    dot_general x3, matrix products, grid_terms(): jnp.einsum('svic,sc->ivs', received_jac, weighted, preferred_element_type...  27.9 us
  transfers between devices with their start and end apart: 5, of which 4 were waited for; matrix products, arithmetic and copies ran while one was open for 3% of the time, Pallas kernels for 0%

commit v1 on v0

v1 whole, which is shorter than its diff:
```python
import functools

import jax
import jax.numpy as jnp
from jax import lax
from jax.experimental import pallas as pl
from jax.experimental.pallas import tpu as pltpu
from jax.sharding import PartitionSpec as P

MESH = pl.DeviceIdType.MESH
HIGHEST = lax.Precision.HIGHEST
COLS = 512
SLAB = 64
ROWS = 40
GROUP = 8
COL_LANE = 63
SUM_LANE = 40


def nt(a, b, precision=None):
    return lax.dot_general(
        a, b, (((1,), (1,)), ((), ())), precision=precision, preferred_element_type=jnp.float32
    )


def nn(a, b, precision=None):
    return lax.dot_general(
        a, b, (((1,), (0,)), ((), ())), precision=precision, preferred_element_type=jnp.float32
    )


def split(x):
    high = x.astype(jnp.bfloat16)
    return high, (x - high.astype(jnp.float32)).astype(jnp.bfloat16)


def iota(shape, dim):
    return lax.broadcasted_iota(jnp.int32, shape, dim)


def kernel(
    tiles,
    bands,
    jac,
    meta,
    innovation,
    precision_off,
    vertical,
    increment,
    residual,
    jpad,
    rmat,
    coef,
    picks,
    sends,
    equal,
    tbuf,
    ibuf,
    sbuf,
    rbuf,
    w0_buf,
    im0_buf,
    w1_buf,
    im1_buf,
    t_send,
    t_recv,
    i_send,
    i_recv,
    s_send,
    s_recv,
):
    me = lax.axis_index("horiz")
    lev = lax.axis_index("lev")
    obs = innovation.shape[0]
    channels = innovation.shape[1]
    slabs, band, _ = jac.shape
    levels = vertical.shape[1]
    f32, bf16 = jnp.float32, jnp.bfloat16

    barrier = pltpu.get_barrier_semaphore()

    @pl.loop(1, tiles)
    def _(k):
        peer = lax.rem(me + k, tiles)
        pl.semaphore_signal(barrier, inc=1, device_id={"horiz": peer}, device_id_type=MESH)

    for k in range(1, bands):
        peer = lax.rem(lev + k, bands)
        pl.semaphore_signal(barrier, inc=1, device_id={"lev": peer}, device_id_type=MESH)

    @pl.loop(0, slabs, unroll=8)
    def _(s):
        start = pl.multiple_of(s * SLAB, SLAB)
        jpad[pl.ds(start + 32, 32), :] = jnp.zeros((32, channels), bf16)
        jpad[pl.ds(start, band), :] = jac[s]

    tile_of = meta[:, 0:1]
    column_of = meta[:, 1:2]
    weight = meta[:, 2:3]
    onehot = (tile_of == iota((obs, tiles), 1).astype(f32)).astype(f32)
    same = nt(onehot.astype(bf16), onehot.astype(bf16))
    earlier = iota((obs, obs), 1) < iota((obs, obs), 0)
    position = jnp.sum(jnp.where(earlier, same, 0.0), axis=1, keepdims=True)
    first = jnp.where(position < 0.5, onehot, 0.0)
    second = jnp.where(position > 0.5, onehot, 0.0)
    picks[:, 0:tiles] = first.astype(bf16)
    picks[:, tiles : 2 * tiles] = second.astype(bf16)
    sends[0:tiles, :] = jnp.concatenate([first, first], axis=0).T.astype(bf16)
    sends[tiles : 2 * tiles, :] = jnp.concatenate([second, second], axis=0).T.astype(bf16)

    off = precision_off[...]
    eye_c = (iota((channels, channels), 0) == iota((channels, channels), 1)).astype(f32)
    rmat[...] = eye_c + 0.5 * (off + off.T)
    row = iota((SLAB, levels), 0)
    own = ((iota((SLAB, levels), 1) == lev * band + row) & (row < band)).astype(f32)
    spread_row = iota((levels, bands * ROWS), 0)
    spread_lane = iota((levels, bands * ROWS), 1)
    spread = jnp.zeros((levels, bands * ROWS), f32)
    for m in range(bands):
        level = spread_lane - m * ROWS
        spread += (
            (level >= 0) & (level < band) & (spread_row == m * band + level)
        ).astype(f32)
    eye_l = (iota((levels, levels), 0) == iota((levels, levels), 1)).astype(f32)
    for v in range(2):
        factor = eye_l + vertical[v]
        both = nt(nn(own, factor, HIGHEST), factor, HIGHEST)
        back = nt(own, factor, HIGHEST)
        coef[v * SLAB : (v + 1) * SLAB, :] = nn(both, spread, HIGHEST)
        coef[(2 + v) * SLAB : (3 + v) * SLAB, :] = nn(back, spread, HIGHEST)

    def weigh(values):
        return weight * nn(values, rmat[...], HIGHEST)

    def adjoint(use, high, low):
        both = jnp.concatenate([high, low], axis=0)
        lane = lax.rem(iota((ROWS, 2 * obs), 1), obs)

        def step(g, sums):
            start = pl.multiple_of(g * (2 * GROUP * SLAB), 2 * GROUP * SLAB)
            product = nt(jpad[pl.ds(start, 2 * GROUP * SLAB), :], both)
            sums = list(sums)
            for j in range(GROUP):
                mine = lane == g * GROUP + j
                for v in range(2):
                    at = (2 * j + v) * SLAB
                    sums[v] = sums[v] + jnp.where(mine, product[at : at + ROWS, :], 0.0)
            return tuple(sums)

        zero = jnp.zeros((ROWS, 2 * obs), f32)
        t0, t1 = lax.fori_loop(0, obs // GROUP, step, (zero, zero))
        t0 = t0 + pltpu.roll(t0, obs, 1)
        t1 = t1 + pltpu.roll(t1, obs, 1)
        tbuf[use, lev] = jnp.where(iota((ROWS, 2 * obs), 1) < obs, t0, t1)

    def between_bands(buf, use, send_sem, recv_sem):
        copies = []
        for k in range(1, bands):
            copy = pltpu.make_async_remote_copy(
                src_ref=buf.at[use, lev],
                dst_ref=buf.at[use, lev],
                send_sem=send_sem.at[use, k],
                recv_sem=recv_sem.at[use, k],
                device_id={"lev": lax.rem(lev + k, bands)},
                device_id_type=MESH,
            )
            copy.start()
            copies.append(copy)
        for copy in copies:
            copy.wait()

    def columns(use):
        gathered = tbuf[use].reshape(bands * ROWS, 2 * obs)
        mapped = nn(coef[...], gathered, HIGHEST)
        diagonal = iota((2 * SLAB, 2 * obs), 0) // SLAB == iota((2 * SLAB, 2 * obs), 1) // obs
        out = []
        for part in range(2):
            block = jnp.where(diagonal, mapped[part * 2 * SLAB : (part + 1) * 2 * SLAB, :], 0.0)
            high, low = split(block)
            slots = nt(sends[...], jnp.concatenate([high, low], axis=0))
            out.append(slots[:, 0 : 2 * SLAB] + slots[:, 2 * SLAB :])
        return out

    def exchange(use):
        @pl.loop(1, tiles)
        def _(k):
            peer = lax.rem(me + k, tiles)
            pltpu.make_async_remote_copy(
                src_ref=sbuf.at[use, peer],
                dst_ref=rbuf.at[use, me],
                send_sem=s_send.at[use],
                recv_sem=s_recv.at[use],
                device_id={"horiz": peer},
                device_id_type=MESH,
            ).start()

        rbuf[use, me] = sbuf[use, me]

    def arrived(use):
        part = rbuf.at[use, pl.ds(0, tiles - 1)]
        pltpu.make_async_copy(part, part, s_recv.at[use]).wait()

    def left(use):
        part = sbuf.at[use, pl.ds(0, tiles - 1)]
        pltpu.make_async_copy(part, part, s_send.at[use]).wait()

    def put(use, slots):
        sbuf[use, :, 0, :] = slots[0:tiles, :]
        sbuf[use, :, 1, :] = slots[tiles : 2 * tiles, :]

    def got(use):
        return jnp.concatenate([rbuf[use, :, 0, :], rbuf[use, :, 1, :]], axis=0)

    def sum_at_tiles(use, first_time):
        slots = got(use)
        if first_time:
            ids = [slots[s * tiles : (s + 1) * tiles, COL_LANE : COL_LANE + 1] for s in range(2)]
            wide = [jnp.broadcast_to(one, (tiles, tiles)) for one in ids]
            tall = [one.T for one in wide]
            for a in range(2):
                for b in range(2):
                    equal[a * tiles : (a + 1) * tiles, b * tiles : (b + 1) * tiles] = jnp.where(
                        (wide[a] == tall[b]) & (wide[a] > 0.5), 1.0, 0.0
                    ).astype(bf16)
        high, low = split(slots)
        sums = nn(equal[...], jnp.concatenate([high, low], axis=1))
        put(use + 1, sums[:, 0 : 2 * SLAB] + sums[:, 2 * SLAB :])
        return slots

    def images(use, from_use):
        high, low = split(got(from_use))
        chosen = nn(picks[...], jnp.concatenate([high, low], axis=1))
        group_row = lax.rem(iota((2 * GROUP, 2 * SLAB), 0), GROUP)
        for g in range(obs // GROUP):
            rows = chosen[g * GROUP : (g + 1) * GROUP, :]
            pair = jnp.concatenate([rows[:, 0 : 2 * SLAB], rows[:, 2 * SLAB :]], axis=0)
            lhs = jnp.concatenate(
                [jnp.where(group_row == j, pair, 0.0) for j in range(GROUP)], axis=1
            ).astype(bf16)
            start = g * 2 * GROUP * SLAB
            part = nn(lhs, jpad[start : start + 2 * GROUP * SLAB, :])
            ibuf[use, lev, g * GROUP : (g + 1) * GROUP, :] = part[0:GROUP, :] + part[GROUP:, :]
        between_bands(ibuf, use, i_send, i_recv)
        total = ibuf[use, 0]
        for m in range(1, bands):
            total = total + ibuf[use, m]
        return total

    w0 = weigh(innovation[...]).astype(bf16)
    w0_buf[...] = w0.astype(f32)
    adjoint(0, w0, jnp.zeros_like(w0))
    pl.semaphore_wait(barrier, tiles - 1 + bands - 1)
    between_bands(tbuf, 0, t_send, t_recv)
    c0, u0 = columns(0)
    column_rhs = jnp.where(
        (iota((2 * obs, 2 * SLAB), 1) == COL_LANE) & (iota((2 * obs, 2 * SLAB), 0) < obs),
        jnp.concatenate([column_of, column_of], axis=0) + 1.0,
        0.0,
    )
    high, low = split(column_rhs)
    put(0, c0 + nn(sends[...], high) + nn(sends[...], low))
    exchange(0)
    put(4, u0)
    arrived(0)
    first_slots = sum_at_tiles(0, True)
    exchange(1)
    exchange(4)
    slot_column = first_slots[:, COL_LANE : COL_LANE + 1]
    arrived(1)
    im0 = images(0, 1)
    im0_buf[...] = im0
    w1 = weigh(im0)
    w1_buf[...] = w1
    adjoint(1, *split(w1))
    between_bands(tbuf, 1, t_send, t_recv)
    c1, u1 = columns(1)
    put(2, c1)
    exchange(2)
    put(5, u1)
    arrived(2)
    sum_at_tiles(2, False)
    exchange(3)
    exchange(5)
    arrived(3)
    im1 = images(1, 3)
    w2 = weigh(im1)
    adjoint(2, *split(w2))
    between_bands(tbuf, 2, t_send, t_recv)
    _, u2 = columns(2)

    w0, im0, w1 = w0_buf[...], im0_buf[...], w1_buf[...]
    lane = iota((1, 2 * SLAB), 1)
    scalars = jnp.zeros((1, 2 * SLAB), f32)
    for at, (a, b) in enumerate(((w0, im0), (w1, im0), (w1, im1), (w2, im0), (w2, im1))):
        one = jnp.sum(jnp.sum(a * b, axis=1, keepdims=True), axis=0, keepdims=True)
        scalars = scalars + jnp.where(lane == SUM_LANE + at, one, 0.0)
    put(6, u2 + scalars)
    exchange(6)
    arrived(4)
    arrived(5)
    arrived(6)
    u2 = got(6)
    sums = jnp.sum(u2[0:tiles, :], axis=0, keepdims=True)
    g00, g01, g11, g02, g12 = (
        jnp.sum(jnp.where(lane == SUM_LANE + at, sums, 0.0), axis=1, keepdims=True)
        for at in range(5)
    )
    a0 = g00 / (g00 + g01)
    keep = 1.0 - a0
    rr1 = keep * keep * g00 - 2.0 * a0 * keep * g01 + a0 * a0 * g11
    k0 = keep + rr1 / g00
    k1 = -a0
    mixed = k0 + k1
    curvature = k0 * k0 * g00 + k0 * (mixed + k1) * g01 + k0 * k1 * g02 + k1 * mixed * g11
    a1 = rr1 / (curvature + k1 * k1 * g12)
    u0, u1 = got(4), got(5)
    place = (slot_column - 1.0 == iota((2 * tiles, COLS), 1).astype(f32)).astype(bf16)
    for out, slots in (
        (increment, (a0 + a1 * k0) * u0 + a1 * k1 * u1),
        (residual, (keep - a1 * k0) * u0 - (a0 + a1 * mixed) * u1 - a1 * k1 * u2),
    ):
        turned = jnp.concatenate([slots[0:tiles, :].T, slots[tiles:, :].T], axis=1)
        high, low = split(turned)
        field = nn(jnp.concatenate([high, low], axis=0), place)
        field = field[0 : 2 * SLAB, :] + field[2 * SLAB :, :]
        out[:, 0, :] = field[0:band, :]
        out[:, 1, :] = field[SLAB : SLAB + band, :]
    for use in range(7):
        left(use)


def shards(
    tiles,
    bands,
    jacobian,
    obs_tile,
    obs_column,
    obs_weight,
    innovation,
    precision_off,
    vertical_factor,
):
    obs, variables, band, channels = jacobian.shape
    f32, bf16 = jnp.float32, jnp.bfloat16
    meta = jnp.concatenate(
        [obs_tile.astype(f32), obs_column.astype(f32)[:, None], obs_weight[:, None]], axis=1
    )
    vmem = pl.BlockSpec(memory_space=pltpu.VMEM)
    out = jax.ShapeDtypeStruct((band, variables, COLS), f32)
    dma = pltpu.SemaphoreType.DMA
    return pl.pallas_call(
        functools.partial(kernel, tiles, bands),
        out_shape=(out, out),
        in_specs=[vmem] * 5,
        out_specs=(vmem, vmem),
        scratch_shapes=[
            pltpu.VMEM((obs * variables * SLAB, channels), bf16),
            pltpu.VMEM((channels, channels), f32),
            pltpu.VMEM((4 * SLAB, bands * ROWS), f32),
            pltpu.VMEM((obs, 2 * tiles), bf16),
            pltpu.VMEM((2 * tiles, 2 * obs), bf16),
            pltpu.VMEM((2 * tiles, 2 * tiles), bf16),
            pltpu.VMEM((3, bands, ROWS, 2 * obs), f32),
            pltpu.VMEM((2, bands, obs, channels), f32),
            pltpu.VMEM((7, tiles, 2, 2 * SLAB), f32),
            pltpu.VMEM((7, tiles, 2, 2 * SLAB), f32),
            pltpu.VMEM((obs, channels), f32),
            pltpu.VMEM((obs, channels), f32),
            pltpu.VMEM((obs, channels), f32),
            pltpu.VMEM((obs, channels), f32),
            dma((3, bands)),
            dma((3, bands)),
            dma((2, bands)),
            dma((2, bands)),
            dma((7,)),
            dma((7,)),
        ],
        compiler_params=pltpu.CompilerParams(
            collective_id=0, has_side_effects=True, vmem_limit_bytes=48 << 20
        ),
        name="analysis",
    )(
        jacobian.reshape(obs * variables, band, channels),
        meta,
        innovation,
        precision_off,
        vertical_factor,
    )


def solution(mesh):
    return jax.shard_map(
        functools.partial(shards, mesh.shape["horiz"], mesh.shape["lev"]),
        mesh=mesh,
        in_specs=(
            P("horiz", None, "lev", None),
            P("horiz", None),
            P("horiz"),
            P("horiz"),
            P("horiz", None),
            P(),
            P(),
        ),
        out_specs=(P("lev", None, "horiz"), P("lev", None, "horiz")),
        check_vma=False,
    )
```

time: 970 us -> 101 us (0.10)
  blocking collectives: 437 us -> 0 us
  waiting for transfers between devices: 380 us -> 0 us
  Pallas kernels: 0 us -> 94.5 us
  matrix products: 45.8 us -> 0 us
  starting transfers between devices: 40.8 us -> 0 us
  local copies, waits for them, and re-layouts: 35 us -> 3.49 us
  between operations: 18.8 us -> 0.7 us
    psum x3 -> x0, blocking collectives: 287 us -> none  [global_sum(): return lax.psum(values, ('horiz', 'lev'))]
    all_to_all x3 -> x0, waiting for transfers between devices: 260 us -> none  [the longest x1 254 us: shards(): lax.all_to_all(jac_buffer, 'horiz', split_axis=0, concat_axis=0, tiled=True)]
    psum x2 -> x0, waiting for transfers between devices: 120 us -> none  [shards(): lax.psum(jnp.einsum('svic,ivs->sc', received_jac, sent, preferred_element...]
    all_to_all x4 -> x0, blocking collectives: 99 us -> none  [the longest x2 63.3 us: shards(): lax.all_to_all(images, 'horiz', split_axis=0, concat_axis=0, tiled=True)]
    pallas_call x0 -> x1, Pallas kernels: none -> 94.5 us  [shards(): pl.pallas_call(functools.partial(kernel, tiles, bands), out_shape=(out, o...]
    all_gather x5 -> x0, blocking collectives: 51.8 us -> none  [vertical(): lax.all_gather(column_field, 'lev', axis=0, tiled=True)]
    dot_general x16 -> x0, matrix products: 45.8 us -> none  [the longest x3 27.9 us: grid_terms(): jnp.einsum('svic,sc->ivs', received_jac, weighted, preferred_element_type...]
    all_to_all x3 -> x0, starting transfers between devices: 40.6 us -> none  [the longest x1 18.4 us: shards(): lax.all_to_all(slot_column, 'horiz', split_axis=0, concat_axis=0, tiled=T...]
  transfers between devices with their start and end apart: 5 -> 0, of which waited for: 4 -> 0; matrix products, arithmetic and copies ran while one was open for 3% -> 0% of each run, Pallas kernels for 0% -> 0%
where the time goes in v1:
time: 101 us
  Pallas kernels  94.5 us (94%)
  local copies, waits for them, and re-layouts  3.49 us (3%)
  other arithmetic  2.03 us (2%)
    pallas_call x1, Pallas kernels, shards(): pl.pallas_call(functools.partial(kernel, tiles, bands), out_shape=(out, o...  94.5 us
    unnamed x9, local copies, waits for them, and re-layouts  3.39 us

profile of v1, /device:TPU:1, one launch (start us, length us, event | category | flops | bytes accessed | tf_op | source)
XLA Modules:
  0.0 100.7 jit_solution(8715106310101057019)
XLA Ops:
  0.6 0.0 copy-start
  0.6 0.0 copy-start.1
  0.7 0.0 copy-start.2
  0.7 0.7 convert_element_type.6
  1.4 0.7 convert_bitcast_fusion
  2.0 0.7 pad_maximum_fusion
  2.7 0.1 copy.14.meta
  2.8 2.1 %copy.13 = bf16[64,2,34,200]{3,2,1,0:T(8,128)(2,1)S(1)} copy(bf16[64,2,34,200]{3,1,2,0:T(2,128)(2,1)} %param.7) | data formatting | bytes 3481600 | tf_op args[0]
  4.9 0.0 copy-done
  4.9 0.0 copy-done.1
  4.9 0.0 copy-done.2
  4.9 94.5 %analysis.1 = (f32[34,2,512]{2,1,0:T(2,128)S(1)}, f32[34,2,512]{2,1,0:T(2,128)S(1)}) custom-call(bf16[128,34,200]{2,1,0:T(8,128)(2,1)S(1)} %bitcast.4, f32[64,3]{1,0:T(8,128)S(1)} %copy.14.meta, f32[64,200]{1,0:T(8,128)S(1)} %copy-done.2, f32[200,200]{1,0:T(8,128)S(1)} %copy-done.1, f32[2,136,136]{2,1,0:T(8,128)S(1)} %copy-done), custom_call_target="tpu_custom_call" | custom-call | tf_op jit(solution)/shard_map/analysis/pallas_call | solution.py:351
  99.4 0.7 copy.17
  100.0 0.7 copy.18
Async XLA Ops:
  0.6 4.2 %copy-start = (f32[2,136,136]{2,1,0:T(8,128)S(1)}, f32[2,136,136]{2,1,0:T(8,128)}, u32[]{:S(2)}) copy-start(f32[2,136,136]{2,1,0:T(8,128)} %vertical.1) | copy-start | bytes 443908
  0.6 4.2 %copy-start.1 = (f32[200,200]{1,0:T(8,128)S(1)}, f32[200,200]{1,0:T(8,128)}, u32[]{:S(2)}) copy-start(f32[200,200]{1,0:T(8,128)} %precision_off.1) | copy-start | bytes 480004
  0.7 4.2 %copy-start.2 = (f32[64,200]{1,0:T(8,128)S(1)}, f32[64,200]{1,0:T(8,128)}, u32[]{:S(2)}) copy-start(f32[64,200]{1,0:T(8,128)} %innovation.1) | copy-start | bytes 153604

commit v2 on v1

v2 whole, which is shorter than its diff:
```python
import functools

import jax
import jax.numpy as jnp
from jax import lax
from jax.experimental import pallas as pl
from jax.experimental.pallas import tpu as pltpu
from jax.sharding import PartitionSpec as P

MESH = pl.DeviceIdType.MESH
HIGHEST = lax.Precision.HIGHEST
COLS = 512
LANES = 128
SLAB = 80
HALF = SLAB // 2
GROUP = 8
COL_LANE = 127
SUM_LANE = 100
RING = 8
CORES = 2


def nt(a, b, precision=None):
    return lax.dot_general(
        a, b, (((1,), (1,)), ((), ())), precision=precision, preferred_element_type=jnp.float32
    )


def nn(a, b, precision=None):
    return lax.dot_general(
        a, b, (((1,), (0,)), ((), ())), precision=precision, preferred_element_type=jnp.float32
    )


def split(x):
    high = x.astype(jnp.bfloat16)
    return high, (x - high.astype(jnp.float32)).astype(jnp.bfloat16)


def iota(shape, dim):
    return lax.broadcasted_iota(jnp.int32, shape, dim)


def far_first(j):
    return lax.rem(RING // 2 + (1 - 2 * lax.rem(j, 2)) * ((j + 1) // 2) + RING, RING)


def for_peers(me, tiles, body):
    here_z, here_y, here_core = me // (RING * CORES), lax.rem(me // CORES, RING), lax.rem(me, CORES)

    @pl.loop(0, tiles - 1)
    def _(k):
        step = k // CORES
        z = lax.rem(here_z + far_first(step // RING), RING)
        y = lax.rem(here_y + far_first(lax.rem(step, RING)), RING)
        core = lax.rem(here_core + 1 + lax.rem(k, CORES), CORES)
        body((z * RING + y) * CORES + core)


def kernel(
    tiles,
    bands,
    jac,
    tile_in,
    column_in,
    weight_in,
    innovation_in,
    precision_in,
    vertical_in,
    increment,
    residual,
    jraw,
    tile_row,
    column_row,
    weight_row,
    innovation,
    precision_off,
    vertical,
    jpad,
    rmat,
    coef_high,
    coef_low,
    picks,
    sends,
    equal,
    repeat,
    tbuf,
    ibuf,
    sbuf,
    rbuf,
    w0_buf,
    im0_buf,
    w1_buf,
    in_sem,
    t_send,
    t_recv,
    i_send,
    i_recv,
    s_send,
    s_recv,
):
    me = lax.axis_index("horiz")
    lev = lax.axis_index("lev")
    obs, channels = innovation.shape
    band = jac.shape[1]
    levels = vertical.shape[1]
    used = 2 * band
    f32, bf16 = jnp.float32, jnp.bfloat16

    fetches = [
        pltpu.make_async_copy(source, target, in_sem.at[at])
        for at, (source, target) in enumerate(
            (
                (innovation_in, innovation),
                (precision_in, precision_off),
                (weight_in, weight_row),
                (tile_in, tile_row),
                (column_in, column_row),
                (jac, jraw),
                (vertical_in, vertical),
            )
        )
    ]
    for fetch in fetches:
        fetch.start()
    barrier = pltpu.get_barrier_semaphore()
    for k in range(1, bands):
        peer = lax.rem(lev + k, bands)
        pl.semaphore_signal(barrier, inc=1, device_id={"lev": peer}, device_id_type=MESH)

    def greet(peer):
        pl.semaphore_signal(barrier, inc=1, device_id={"horiz": peer}, device_id_type=MESH)

    for_peers(me, tiles, greet)

    def column(row):
        return jnp.broadcast_to(row[...].astype(f32), (obs, obs)).T[:, 0:1]

    for fetch in fetches[:5]:
        fetch.wait()
    weight = column(weight_row)
    off = precision_off[...]
    eye_c = (iota((channels, channels), 0) == iota((channels, channels), 1)).astype(f32)
    rmat[...] = eye_c + 0.5 * (off + off.T)

    def weigh(values):
        return weight * nn(values, rmat[...], HIGHEST)

    w0 = weigh(innovation[...]).astype(bf16)
    w0_buf[...] = w0.astype(f32)

    fetches[5].wait()

    @pl.loop(0, obs, unroll=4)
    def _(o):
        start = pl.multiple_of(o * SLAB, 16)
        jpad[pl.ds(start + 64, 16), :] = jnp.zeros((16, channels), bf16)
        jpad[pl.ds(start, used), :] = jraw[o].reshape(used, channels)

    def adjoint(use, high, low):
        both = jnp.concatenate([high, low], axis=0)
        lane = lax.rem(iota((SLAB, 2 * obs), 1), obs)

        def step(g, total):
            start = pl.multiple_of(g * (GROUP * SLAB), 16)
            product = nt(jpad[pl.ds(start, GROUP * SLAB), :], both)
            for j in range(GROUP):
                mine = lane == g * GROUP + j
                total = total + jnp.where(mine, product[j * SLAB : (j + 1) * SLAB, :], 0.0)
            return total

        t = lax.fori_loop(0, obs // GROUP, step, jnp.zeros((SLAB, 2 * obs), f32), unroll=8)
        t = t + pltpu.roll(t, obs, 1)
        tbuf[use, lev] = jnp.where(iota((HALF, 2 * obs), 1) < obs, t[0:HALF, :], t[HALF:, :])

    adjoint(0, w0, jnp.zeros_like(w0))

    onehot = (column(tile_row) == iota((obs, tiles), 1).astype(f32)).astype(f32)
    same = nt(onehot.astype(bf16), onehot.astype(bf16))
    earlier = iota((obs, obs), 1) < iota((obs, obs), 0)
    position = jnp.sum(jnp.where(earlier, same, 0.0), axis=1, keepdims=True)
    first = jnp.where(position < 0.5, onehot, 0.0)
    second = jnp.where(position > 0.5, onehot, 0.0)
    picks[:, 0:tiles] = first.astype(bf16)
    picks[:, tiles : 2 * tiles] = second.astype(bf16)
    nothing = jnp.zeros((obs, tiles), f32)
    sends[0:tiles, :] = jnp.concatenate([first, nothing], axis=0).T.astype(bf16)
    sends[tiles : 2 * tiles, :] = jnp.concatenate([second, nothing], axis=0).T.astype(bf16)
    repeat[...] = (
        iota((LANES, GROUP * SLAB), 0) == lax.rem(iota((LANES, GROUP * SLAB), 1), SLAB)
    ).astype(bf16)

    fetches[6].wait()

    row = iota((LANES, levels), 0)
    wide = iota((levels, 2 * bands * HALF), 1)
    places = lax.rem(wide, HALF) + (wide // (bands * HALF)) * HALF
    wide_level = lax.rem(wide // HALF, bands) * band + places // 2
    inside = (places < used) & (wide_level == iota(wide.shape, 0))
    eye_l = (iota((levels, levels), 0) == iota((levels, levels), 1)).astype(f32)
    both, back = 0.0, 0.0
    for v in range(2):
        factor = eye_l + vertical[v]
        own = (iota(row.shape, 1) == lev * band + row // 2) & (row < used) & (lax.rem(row, 2) == v)
        spread = jnp.where(inside & (lax.rem(places, 2) == v), 1.0, 0.0)
        own = own.astype(f32)
        both = both + nn(nt(nn(own, factor, HIGHEST), factor, HIGHEST), spread, HIGHEST)
        back = back + nn(nt(own, factor, HIGHEST), spread, HIGHEST)
    coef_high[0:LANES, :], coef_low[0:LANES, :] = split(both)
    coef_high[LANES:, :], coef_low[LANES:, :] = split(back)

    def band_copies(buf, use, send_sem, recv_sem, part, rows):
        copies = []
        for k in range(1, bands):
            copy = pltpu.make_async_remote_copy(
                src_ref=buf.at[use, lev, rows],
                dst_ref=buf.at[use, lev, rows],
                send_sem=send_sem.at[use, part, k],
                recv_sem=recv_sem.at[use, part, k],
                device_id={"lev": lax.rem(lev + k, bands)},
                device_id_type=MESH,
            )
            copy.start()
            copies.append(copy)
        return copies

    def gather_bands(use):
        return band_copies(tbuf, use, t_send, t_recv, 0, pl.ds(0, HALF))

    def columns(use, part):
        gathered = tbuf[use].reshape(bands * HALF, 2 * obs)
        gathered = jnp.concatenate([gathered, pltpu.roll(gathered, obs, 1)], axis=0)
        high, low = split(gathered)
        rows = pl.ds(part * LANES, LANES)
        mapped = nn(coef_high[rows, :], high) + (
            nn(coef_high[rows, :], low) + nn(coef_low[rows, :], high)
        )
        mapped = jnp.where(iota((LANES, 2 * obs), 1) < obs, mapped, 0.0)
        high, low = split(mapped)
        slots = nt(sends[...], jnp.concatenate([high, low], axis=0))
        return slots[:, 0:LANES] + slots[:, LANES:]

    def exchange(use):
        def send(peer):
            pltpu.make_async_remote_copy(
                src_ref=sbuf.at[use, peer],
                dst_ref=rbuf.at[use, me],
                send_sem=s_send.at[use],
                recv_sem=s_recv.at[use],
                device_id={"horiz": peer},
                device_id_type=MESH,
            ).start()

        for_peers(me, tiles, send)
        rbuf[use, me] = sbuf[use, me]

    def arrived(use):
        part = rbuf.at[use, pl.ds(0, tiles - 1)]
        pltpu.make_async_copy(part, part, s_recv.at[use]).wait()

    def left(use):
        part = sbuf.at[use, pl.ds(0, tiles - 1)]
        pltpu.make_async_copy(part, part, s_send.at[use]).wait()

    def put(use, slots):
        sbuf[use, :, 0, :] = slots[0:tiles, :]
        sbuf[use, :, 1, :] = slots[tiles : 2 * tiles, :]

    def got(use):
        return jnp.concatenate([rbuf[use, :, 0, :], rbuf[use, :, 1, :]], axis=0)

    def sum_at_tiles(use, first_time):
        slots = got(use)
        if first_time:
            ids = [slots[s * tiles : (s + 1) * tiles, COL_LANE : COL_LANE + 1] for s in range(2)]
            wide = [jnp.broadcast_to(one, (tiles, tiles)) for one in ids]
            tall = [one.T for one in wide]
            for a in range(2):
                for b in range(2):
                    equal[a * tiles : (a + 1) * tiles, b * tiles : (b + 1) * tiles] = jnp.where(
                        (wide[a] == tall[b]) & (wide[a] > 0.5), 1.0, 0.0
                    ).astype(bf16)
        high, low = split(slots)
        sums = nn(equal[...], jnp.concatenate([high, low], axis=1))
        put(use + 1, sums[:, 0:LANES] + sums[:, LANES:])
        return slots

    def images(use, from_use):
        high, low = split(got(from_use))
        chosen = nn(picks[...], jnp.concatenate([high, low], axis=1)).astype(bf16)
        chosen = jnp.concatenate([chosen[:, 0:LANES], chosen[:, LANES:]], axis=0)
        spread = nn(chosen, repeat[...])
        shape = (2 * obs, GROUP * SLAB)
        spread = jnp.where(lax.rem(iota(shape, 0), GROUP) == iota(shape, 1) // SLAB, spread, 0.0)
        copies = []
        half = obs // GROUP // 2
        for g in range(obs // GROUP):
            at = g * GROUP
            lhs = jnp.concatenate(
                [spread[at : at + GROUP, :], spread[obs + at : obs + at + GROUP, :]], axis=0
            )
            part = nn(lhs.astype(bf16), jpad[at * SLAB : (at + GROUP) * SLAB, :])
            ibuf[use, lev, at : at + GROUP, :] = part[0:GROUP, :] + part[GROUP:, :]
            if g == half - 1 or g == 2 * half - 1:
                p = g // half
                rows = pl.ds(p * half * GROUP, half * GROUP)
                copies += band_copies(ibuf, use, i_send, i_recv, p, rows)
        for copy in copies:
            copy.wait()
        total = ibuf[use, 0]
        for m in range(1, bands):
            total = total + ibuf[use, m]
        return total

    def wait_all(copies):
        for copy in copies:
            copy.wait()

    pl.semaphore_wait(barrier, tiles - 1 + bands - 1)
    copies = gather_bands(0)
    column_rhs = jnp.concatenate([column(column_row) + 1.0, jnp.zeros((obs, 1), f32)], axis=0)
    column_rhs = jnp.where(iota((2 * obs, LANES), 1) == COL_LANE, column_rhs, 0.0)
    high, low = split(column_rhs)
    column_slots = nn(sends[...], high) + nn(sends[...], low)
    wait_all(copies)
    put(0, columns(0, 0) + column_slots)
    exchange(0)
    put(4, columns(0, 1))
    arrived(0)
    first_slots = sum_at_tiles(0, True)
    exchange(1)
    exchange(4)
    slot_column = first_slots[:, COL_LANE : COL_LANE + 1]
    arrived(1)
    im0 = images(0, 1)
    im0_buf[...] = im0
    w1 = weigh(im0)
    w1_buf[...] = w1
    adjoint(1, *split(w1))
    wait_all(gather_bands(1))
    put(2, columns(1, 0))
    exchange(2)
    put(5, columns(1, 1))
    arrived(2)
    sum_at_tiles(2, False)
    exchange(3)
    exchange(5)
    arrived(3)
    im1 = images(1, 3)
    w2 = weigh(im1)
    adjoint(2, *split(w2))
    copies = gather_bands(2)

    w0, im0, w1 = w0_buf[...], im0_buf[...], w1_buf[...]
    lane = iota((1, LANES), 1)
    scalars = jnp.zeros((1, LANES), f32)
    for at, (a, b) in enumerate(((w0, im0), (w1, im0), (w1, im1), (w2, im0), (w2, im1))):
        one = jnp.sum(jnp.sum(a * b, axis=1, keepdims=True), axis=0, keepdims=True)
        scalars = scalars + jnp.where(lane == SUM_LANE + at, one, 0.0)
    wait_all(copies)
    put(6, columns(2, 1) + scalars)
    exchange(6)

    place = (slot_column - 1.0 == iota((2 * tiles, COLS), 1).astype(f32)).astype(bf16)

    def field(slots):
        turned = jnp.concatenate([slots[0:tiles, :].T, slots[tiles:, :].T], axis=1)
        high, low = split(turned[0:SLAB, :])
        out = nn(jnp.concatenate([high, low], axis=0), place)
        return out[0:used, :] + out[SLAB : SLAB + used, :]

    arrived(4)
    increment[...] = field(got(4))
    arrived(5)
    residual[...] = field(got(5))
    arrived(6)
    last = got(6)
    sums = jnp.sum(last[0:tiles, :], axis=0, keepdims=True)
    g00, g01, g11, g02, g12 = (
        jnp.sum(jnp.where(lane == SUM_LANE + at, sums, 0.0), axis=1, keepdims=True)
        for at in range(5)
    )
    a0 = g00 / (g00 + g01)
    keep = 1.0 - a0
    rr1 = keep * keep * g00 - 2.0 * a0 * keep * g01 + a0 * a0 * g11
    k0 = keep + rr1 / g00
    k1 = -a0
    mixed = k0 + k1
    curvature = k0 * k0 * g00 + k0 * (mixed + k1) * g01 + k0 * k1 * g02 + k1 * mixed * g11
    a1 = rr1 / (curvature + k1 * k1 * g12)
    v0, v1, v2 = increment[...], residual[...], field(last)
    increment[...] = (a0 + a1 * k0) * v0 + a1 * k1 * v1
    residual[...] = (keep - a1 * k0) * v0 - (a0 + a1 * mixed) * v1 - a1 * k1 * v2
    for use in range(7):
        left(use)


def shards(
    tiles,
    bands,
    jacobian,
    obs_tile,
    obs_column,
    obs_weight,
    innovation,
    precision_off,
    vertical_factor,
):
    obs, variables, band, channels = jacobian.shape
    f32, bf16 = jnp.float32, jnp.bfloat16
    vmem = pl.BlockSpec(memory_space=pltpu.VMEM)
    out = jax.ShapeDtypeStruct((band * variables, COLS), f32)
    dma = pltpu.SemaphoreType.DMA
    by_level = jnp.transpose(jacobian, (0, 2, 1, 3))
    increment, residual = pl.pallas_call(
        functools.partial(kernel, tiles, bands),
        out_shape=(out, out),
        in_specs=[pl.BlockSpec(memory_space=pl.ANY)] * 7,
        out_specs=(vmem, vmem),
        scratch_shapes=[
            pltpu.VMEM(by_level.shape, bf16),
            pltpu.VMEM((1, obs), jnp.int32),
            pltpu.VMEM((1, obs), jnp.int32),
            pltpu.VMEM((1, obs), f32),
            pltpu.VMEM((obs, channels), f32),
            pltpu.VMEM((channels, channels), f32),
            pltpu.VMEM(vertical_factor.shape, f32),
            pltpu.VMEM((obs * SLAB, channels), bf16),
            pltpu.VMEM((channels, channels), f32),
            pltpu.VMEM((2 * LANES, 2 * bands * HALF), bf16),
            pltpu.VMEM((2 * LANES, 2 * bands * HALF), bf16),
            pltpu.VMEM((obs, 2 * tiles), bf16),
            pltpu.VMEM((2 * tiles, 2 * obs), bf16),
            pltpu.VMEM((2 * tiles, 2 * tiles), bf16),
            pltpu.VMEM((LANES, GROUP * SLAB), bf16),
            pltpu.VMEM((3, bands, HALF, 2 * obs), f32),
            pltpu.VMEM((2, bands, obs, channels), f32),
            pltpu.VMEM((7, tiles, 2, LANES), f32),
            pltpu.VMEM((7, tiles, 2, LANES), f32),
            pltpu.VMEM((obs, channels), f32),
            pltpu.VMEM((obs, channels), f32),
            pltpu.VMEM((obs, channels), f32),
            dma((7,)),
            dma((3, 1, bands)),
            dma((3, 1, bands)),
            dma((2, 2, bands)),
            dma((2, 2, bands)),
            dma((7,)),
            dma((7,)),
        ],
        compiler_params=pltpu.CompilerParams(
            collective_id=0, has_side_effects=True, vmem_limit_bytes=60 << 20
        ),
        name="analysis",
    )(
        by_level,
        obs_tile.reshape(1, obs),
        obs_column.reshape(1, obs),
        obs_weight.reshape(1, obs),
        innovation,
        precision_off,
        vertical_factor,
    )
    shape = (band, variables, COLS)
    return increment.reshape(shape), residual.reshape(shape)


def solution(mesh):
    return jax.shard_map(
        functools.partial(shards, mesh.shape["horiz"], mesh.shape["lev"]),
        mesh=mesh,
        in_specs=(
            P("horiz", None, "lev", None),
            P("horiz", None),
            P("horiz"),
            P("horiz"),
            P("horiz", None),
            P(),
            P(),
        ),
        out_specs=(P("lev", None, "horiz"), P("lev", None, "horiz")),
        check_vma=False,
    )
```

time: 101 us -> 111 us (1.099)
  Pallas kernels: 94.5 us -> 107 us
  other arithmetic: 2.03 us -> 0 us
    pallas_call x1, Pallas kernels: 94.5 us -> 107 us  [shards(): pl.pallas_call(functools.partial(kernel, tiles, bands), out_shape=(out, o...]
    unnamed x9 -> x0, local copies, waits for them, and re-layouts: 3.39 us -> none
    reshape x0 -> x2, local copies, waits for them, and re-layouts: none -> 3.29 us  [shards(): return (increment.reshape(shape), residual.reshape(shape))]
where the time goes in v2:
time: 111 us
  Pallas kernels  107 us (96%)
  local copies, waits for them, and re-layouts  3.29 us (3%)
    pallas_call x1, Pallas kernels, shards(): pl.pallas_call(functools.partial(kernel, tiles, bands), out_shape=(out, o...  107 us
    reshape x2, local copies, waits for them, and re-layouts, shards(): return (increment.reshape(shape), residual.reshape(shape))  3.29 us

profile of v2, /device:TPU:1, one launch (start us, length us, event | category | flops | bytes accessed | tf_op | source)
XLA Modules:
  0.0 110.8 jit_solution(7520474723670627536)
XLA Ops:
  0.6 106.9 %analysis.1 = (f32[68,512]{1,0:T(8,128)}, f32[68,512]{1,0:T(8,128)}) custom-call(bf16[64,34,2,200]{3,2,1,0:T(2,128)(2,1)} %bitcast.4, s32[1,64]{1,0:T(1,128)} %bitcast.5, s32[1,64]{1,0:T(1,128)} %bitcast.6, f32[1,64]{1,0:T(1,128)} %bitcast.7, f32[64,200]{1,0:T(8,128)} %innovation_in.1, f32[200,200]{1,0:T(8,128)} %precision_in.1, f32[2,136,136]{2,1,0:T(8,128)} %vertical_in.1), custom_call_target="tpu_custom_call" | custom-call | tf_op jit(solution)/shard_map/analysis/pallas_call | solution.py:415
  107.5 1.6 %reshape.22 = f32[34,2,512]{2,1,0:T(2,128)} reshape(f32[68,512]{1,0:T(8,128)} %get-tuple-element.4) | data formatting | bytes 278528 | tf_op jit(solution)/shard_map/reshape | solution.py:465
  109.1 1.6 %reshape.23 = f32[34,2,512]{2,1,0:T(2,128)} reshape(f32[68,512]{1,0:T(8,128)} %get-tuple-element.5) | data formatting | bytes 278528 | tf_op jit(solution)/shard_map/reshape | solution.py:465

commit v3 on v2

--- a/solution.py
+++ b/solution.py
@@ -16,8 +16,6 @@
 GROUP = 8
 COL_LANE = 127
 SUM_LANE = 100
-RING = 8
-CORES = 2
 
 
 def nt(a, b, precision=None):
@@ -41,20 +39,14 @@
     return lax.broadcasted_iota(jnp.int32, shape, dim)
 
 
-def far_first(j):
-    return lax.rem(RING // 2 + (1 - 2 * lax.rem(j, 2)) * ((j + 1) // 2) + RING, RING)
-
-
 def for_peers(me, tiles, body):
-    here_z, here_y, here_core = me // (RING * CORES), lax.rem(me // CORES, RING), lax.rem(me, CORES)
-
-    @pl.loop(0, tiles - 1)
+    half = tiles // 2
+    body(lax.rem(me + half, tiles))
+
+    @pl.loop(1, half)
     def _(k):
-        step = k // CORES
-        z = lax.rem(here_z + far_first(step // RING), RING)
-        y = lax.rem(here_y + far_first(lax.rem(step, RING)), RING)
-        core = lax.rem(here_core + 1 + lax.rem(k, CORES), CORES)
-        body((z * RING + y) * CORES + core)
+        body(lax.rem(me + (half + k), tiles))
+        body(lax.rem(me + (half - k), tiles))
 
 
 def kernel(
@@ -88,9 +80,9 @@
     ibuf,
     sbuf,
     rbuf,
-    w0_buf,
-    im0_buf,
-    w1_buf,
+    w_buf,
+    im_buf,
+    fields,
     in_sem,
     t_send,
     t_recv,
@@ -143,11 +135,8 @@
     eye_c = (iota((channels, channels), 0) == iota((channels, channels), 1)).astype(f32)
     rmat[...] = eye_c + 0.5 * (off + off.T)
 
-    def weigh(values):
-        return weight * nn(values, rmat[...], HIGHEST)
-
-    w0 = weigh(innovation[...]).astype(bf16)
-    w0_buf[...] = w0.astype(f32)
+    w0 = (weight * nn(innovation[...], rmat[...], HIGHEST)).astype(bf16)
+    w_buf[0] = w0.astype(f32)
 
     fetches[5].wait()
 
@@ -157,23 +146,47 @@
         jpad[pl.ds(start + 64, 16), :] = jnp.zeros((16, channels), bf16)
         jpad[pl.ds(start, used), :] = jraw[o].reshape(used, channels)
 
-    def adjoint(use, high, low):
-        both = jnp.concatenate([high, low], axis=0)
+    def adjoint(high, low, part, parts, total):
+        groups = obs // GROUP // parts
+        rows = groups * GROUP
+        before = [jnp.zeros((rows, channels), bf16)] * part
+        after = [jnp.zeros((rows, channels), bf16)] * (parts - 1 - part)
+        both = jnp.concatenate([*before, high, *after, *before, low, *after], axis=0)
         lane = lax.rem(iota((SLAB, 2 * obs), 1), obs)
-
-        def step(g, total):
-            start = pl.multiple_of(g * (GROUP * SLAB), 16)
-            product = nt(jpad[pl.ds(start, GROUP * SLAB), :], both)
+        for g in range(part * groups, (part + 1) * groups):
+            product = nt(jpad[g * GROUP * SLAB : (g + 1) * GROUP * SLAB, :], both)
             for j in range(GROUP):
                 mine = lane == g * GROUP + j
                 total = total + jnp.where(mine, product[j * SLAB : (j + 1) * SLAB, :], 0.0)
-            return total
-
-        t = lax.fori_loop(0, obs // GROUP, step, jnp.zeros((SLAB, 2 * obs), f32), unroll=8)
+        return total
+
+    def store_terms(use, t):
         t = t + pltpu.roll(t, obs, 1)
         tbuf[use, lev] = jnp.where(iota((HALF, 2 * obs), 1) < obs, t[0:HALF, :], t[HALF:, :])
 
-    adjoint(0, w0, jnp.zeros_like(w0))
+    no_terms = jnp.zeros((SLAB, 2 * obs), f32)
+    store_terms(0, adjoint(w0, jnp.zeros_like(w0), 0, 1, no_terms))
+
+    def band_copies(buf, use, send_sem, recv_sem, part, rows):
+        copies = []
+        for k in range(1, bands):
+            copy = pltpu.make_async_remote_copy(
+                src_ref=buf.at[use, lev, rows],
+                dst_ref=buf.at[use, lev, rows],
+                send_sem=send_sem.at[use, part, k],
+                recv_sem=recv_sem.at[use, part, k],
+                device_id={"lev": lax.rem(lev + k, bands)},
+                device_id_type=MESH,
+            )
+            copy.start()
+            copies.append(copy)
+        return copies
+
+    def gather_bands(use):
+        return band_copies(tbuf, use, t_send, t_recv, 0, pl.ds(0, HALF))
+
+    pl.semaphore_wait(barrier, tiles - 1 + bands - 1)
+    copies = gather_bands(0)
 
     onehot = (column(tile_row) == iota((obs, tiles), 1).astype(f32)).astype(f32)
     same = nt(onehot.astype(bf16), onehot.astype(bf16))
@@ -209,24 +222,6 @@
     coef_high[0:LANES, :], coef_low[0:LANES, :] = split(both)
     coef_high[LANES:, :], coef_low[LANES:, :] = split(back)
 
-    def band_copies(buf, use, send_sem, recv_sem, part, rows):
-        copies = []
-        for k in range(1, bands):
-            copy = pltpu.make_async_remote_copy(
-                src_ref=buf.at[use, lev, rows],
-                dst_ref=buf.at[use, lev, rows],
-                send_sem=send_sem.at[use, part, k],
-                recv_sem=recv_sem.at[use, part, k],
-                device_id={"lev": lax.rem(lev + k, bands)},
-                device_id_type=MESH,
-            )
-            copy.start()
-            copies.append(copy)
-        return copies
-
-    def gather_bands(use):
-        return band_copies(tbuf, use, t_send, t_recv, 0, pl.ds(0, HALF))
-
     def columns(use, part):
         gathered = tbuf[use].reshape(bands * HALF, 2 * obs)
         gathered = jnp.concatenate([gathered, pltpu.roll(gathered, obs, 1)], axis=0)
@@ -285,7 +280,9 @@
         put(use + 1, sums[:, 0:LANES] + sums[:, LANES:])
         return slots
 
-    def images(use, from_use):
+    parts = 2
+
+    def start_images(use, from_use):
         high, low = split(got(from_use))
         chosen = nn(picks[...], jnp.concatenate([high, low], axis=1)).astype(bf16)
         chosen = jnp.concatenate([chosen[:, 0:LANES], chosen[:, LANES:]], axis=0)
@@ -293,7 +290,7 @@
         shape = (2 * obs, GROUP * SLAB)
         spread = jnp.where(lax.rem(iota(shape, 0), GROUP) == iota(shape, 1) // SLAB, spread, 0.0)
         copies = []
-        half = obs // GROUP // 2
+        groups = obs // GROUP // parts
         for g in range(obs // GROUP):
             at = g * GROUP
             lhs = jnp.concatenate(
@@ -301,23 +298,32 @@
             )
             part = nn(lhs.astype(bf16), jpad[at * SLAB : (at + GROUP) * SLAB, :])
             ibuf[use, lev, at : at + GROUP, :] = part[0:GROUP, :] + part[GROUP:, :]
-            if g == half - 1 or g == 2 * half - 1:
-                p = g // half
-                rows = pl.ds(p * half * GROUP, half * GROUP)
-                copies += band_copies(ibuf, use, i_send, i_recv, p, rows)
-        for copy in copies:
-            copy.wait()
-        total = ibuf[use, 0]
-        for m in range(1, bands):
-            total = total + ibuf[use, m]
-        return total
+            if (g + 1) % groups == 0:
+                p = g // groups
+                rows = pl.ds(p * groups * GROUP, groups * GROUP)
+                copies.append(band_copies(ibuf, use, i_send, i_recv, p, rows))
+        return copies
+
+    def weigh_images(use, copies):
+        terms = no_terms
+        size = obs // parts
+        for p in range(parts):
+            wait_all(copies[p])
+            rows = slice(p * size, (p + 1) * size)
+            total = ibuf[use, 0, rows, :]
+            for m in range(1, bands):
+                total = total + ibuf[use, m, rows, :]
+            im_buf[use, rows, :] = total
+            w = weight[rows, :] * nn(total, rmat[...], HIGHEST)
+            w_buf[use + 1, rows, :] = w
+            high, low = split(w)
+            terms = adjoint(high, low, p, parts, terms)
+        store_terms(use + 1, terms)
 
     def wait_all(copies):
         for copy in copies:
             copy.wait()
 
-    pl.semaphore_wait(barrier, tiles - 1 + bands - 1)
-    copies = gather_bands(0)
     column_rhs = jnp.concatenate([column(column_row) + 1.0, jnp.zeros((obs, 1), f32)], axis=0)
     column_rhs = jnp.where(iota((2 * obs, LANES), 1) == COL_LANE, column_rhs, 0.0)
     high, low = split(column_rhs)
@@ -329,14 +335,11 @@
     arrived(0)
     first_slots = sum_at_tiles(0, True)
     exchange(1)
-    exchange(4)
     slot_column = first_slots[:, COL_LANE : COL_LANE + 1]
     arrived(1)
-    im0 = images(0, 1)
-    im0_buf[...] = im0
-    w1 = weigh(im0)
-    w1_buf[...] = w1
-    adjoint(1, *split(w1))
+    copies = start_images(0, 1)
+    exchange(4)
+    weigh_images(0, copies)
     wait_all(gather_bands(1))
     put(2, columns(1, 0))
     exchange(2)
@@ -344,14 +347,14 @@
     arrived(2)
     sum_at_tiles(2, False)
     exchange(3)
+    arrived(3)
+    copies = start_images(1, 3)
     exchange(5)
-    arrived(3)
-    im1 = images(1, 3)
-    w2 = weigh(im1)
-    adjoint(2, *split(w2))
+    weigh_images(1, copies)
     copies = gather_bands(2)
 
-    w0, im0, w1 = w0_buf[...], im0_buf[...], w1_buf[...]
+    w0, w1, w2 = w_buf[0], w_buf[1], w_buf[2]
+    im0, im1 = im_buf[0], im_buf[1]
     lane = iota((1, LANES), 1)
     scalars = jnp.zeros((1, LANES), f32)
     for at, (a, b) in enumerate(((w0, im0), (w1, im0), (w1, im1), (w2, im0), (w2, im1))):
@@ -370,9 +373,9 @@
         return out[0:used, :] + out[SLAB : SLAB + used, :]
 
     arrived(4)
-    increment[...] = field(got(4))
+    fields[0] = field(got(4))
     arrived(5)
-    residual[...] = field(got(5))
+    fields[1] = field(got(5))
     arrived(6)
     last = got(6)
     sums = jnp.sum(last[0:tiles, :], axis=0, keepdims=True)
@@ -388,9 +391,12 @@
     mixed = k0 + k1
     curvature = k0 * k0 * g00 + k0 * (mixed + k1) * g01 + k0 * k1 * g02 + k1 * mixed * g11
     a1 = rr1 / (curvature + k1 * k1 * g12)
-    v0, v1, v2 = increment[...], residual[...], field(last)
-    increment[...] = (a0 + a1 * k0) * v0 + a1 * k1 * v1
-    residual[...] = (keep - a1 * k0) * v0 - (a0 + a1 * mixed) * v1 - a1 * k1 * v2
+    v0, v1, v2 = fields[0], fields[1], field(last)
+    shape = increment.shape
+    increment[...] = ((a0 + a1 * k0) * v0 + a1 * k1 * v1).reshape(shape)
+    residual[...] = (
+        (keep - a1 * k0) * v0 - (a0 + a1 * mixed) * v1 - a1 * k1 * v2
+    ).reshape(shape)
     for use in range(7):
         left(use)
 
@@ -409,7 +415,7 @@
     obs, variables, band, channels = jacobian.shape
     f32, bf16 = jnp.float32, jnp.bfloat16
     vmem = pl.BlockSpec(memory_space=pltpu.VMEM)
-    out = jax.ShapeDtypeStruct((band * variables, COLS), f32)
+    out = jax.ShapeDtypeStruct((band, variables, COLS), f32)
     dma = pltpu.SemaphoreType.DMA
     by_level = jnp.transpose(jacobian, (0, 2, 1, 3))
     increment, residual = pl.pallas_call(
@@ -437,9 +443,9 @@
             pltpu.VMEM((2, bands, obs, channels), f32),
             pltpu.VMEM((7, tiles, 2, LANES), f32),
             pltpu.VMEM((7, tiles, 2, LANES), f32),
-            pltpu.VMEM((obs, channels), f32),
-            pltpu.VMEM((obs, channels), f32),
-            pltpu.VMEM((obs, channels), f32),
+            pltpu.VMEM((3, obs, channels), f32),
+            pltpu.VMEM((2, obs, channels), f32),
+            pltpu.VMEM((2, variables * band, COLS), f32),
             dma((7,)),
             dma((3, 1, bands)),
             dma((3, 1, bands)),
@@ -461,8 +467,7 @@
         precision_off,
         vertical_factor,
     )
-    shape = (band, variables, COLS)
-    return increment.reshape(shape), residual.reshape(shape)
+    return increment, residual
 
 
 def solution(mesh):

time: 111 us -> 86.6 us (0.78)
  Pallas kernels: 107 us -> 82.6 us
    pallas_call x1, Pallas kernels: 107 us -> 82.6 us  [shards(): pl.pallas_call(functools.partial(kernel, tiles, bands), out_shape=(out, o...]
    reshape x2 -> x0, local copies, waits for them, and re-layouts: 3.29 us -> none  [shards(): return (increment.reshape(shape), residual.reshape(shape))]
    unnamed x0 -> x2, local copies, waits for them, and re-layouts: none -> 3.15 us
where the time goes in v3:
time: 86.6 us; the launch traced here: 86.4 us
  Pallas kernels  82.6 us (95%)
  local copies, waits for them, and re-layouts  3.15 us (4%)
    pallas_call x1, Pallas kernels, shards(): pl.pallas_call(functools.partial(kernel, tiles, bands), out_shape=(out, o...  82.6 us
    unnamed x2, local copies, waits for them, and re-layouts  3.15 us

profile of v3, /device:TPU:1, one launch (start us, length us, event | category | flops | bytes accessed | tf_op | source)
XLA Modules:
  0.0 86.4 jit_solution(706298215295386619)
XLA Ops:
  0.6 82.6 %analysis.1 = (f32[34,2,512]{2,1,0:T(2,128)}, f32[34,2,512]{2,1,0:T(2,128)}) custom-call(bf16[64,34,2,200]{3,2,1,0:T(2,128)(2,1)} %bitcast.4, s32[1,64]{1,0:T(1,128)} %bitcast.5, s32[1,64]{1,0:T(1,128)} %bitcast.6, f32[1,64]{1,0:T(1,128)} %bitcast.7, f32[64,200]{1,0:T(8,128)} %innovation_in.1, f32[200,200]{1,0:T(8,128)} %precision_in.1, ...), custom_call_target="tpu_custom_call" | custom-call | tf_op jit(solution)/shard_map/analysis/pallas_call | solution.py:421
  83.3 1.6 %copy.11 = f32[34,2,512]{2,1,0:T(2,128)} copy(f32[34,2,512]{2,1,0:T(2,128)} %get-tuple-element.4) | data formatting | bytes 278528
  84.9 1.6 %copy.12 = f32[34,2,512]{2,1,0:T(2,128)} copy(f32[34,2,512]{2,1,0:T(2,128)} %get-tuple-element.5) | data formatting | bytes 278528

commit v4 on v3

--- a/solution.py
+++ b/solution.py
@@ -14,6 +14,8 @@
 SLAB = 80
 HALF = SLAB // 2
 GROUP = 8
+RING = 8
+CORES = 2
 COL_LANE = 127
 SUM_LANE = 100
 
@@ -39,14 +41,24 @@
     return lax.broadcasted_iota(jnp.int32, shape, dim)
 
 
-def for_peers(me, tiles, body):
-    half = tiles // 2
-    body(lax.rem(me + half, tiles))
-
-    @pl.loop(1, half)
-    def _(k):
-        body(lax.rem(me + (half + k), tiles))
-        body(lax.rem(me + (half - k), tiles))
+def hops(offset):
+    return min(offset, RING - offset)
+
+
+def far_first():
+    offsets = [(z, y) for z in range(RING) for y in range(RING)]
+    return sorted(offsets, key=lambda at: -hops(at[0]) - hops(at[1]))
+
+
+def for_peers(me, body):
+    here_z, here_y, core = me // (RING * CORES), lax.rem(me // CORES, RING), lax.rem(me, CORES)
+    at_z = [lax.rem(here_z + d, RING) * (RING * CORES) for d in range(RING)]
+    at_y = [lax.rem(here_y + d, RING) * CORES for d in range(RING)]
+    for z, y in far_first():
+        chip = at_z[z] + at_y[y]
+        for d in range(CORES):
+            if z or y or d:
+                body(chip + lax.rem(core + d, CORES))
 
 
 def kernel(
@@ -83,6 +95,7 @@
     w_buf,
     im_buf,
     fields,
+    entered,
     in_sem,
     t_send,
     t_recv,
@@ -120,10 +133,14 @@
         peer = lax.rem(lev + k, bands)
         pl.semaphore_signal(barrier, inc=1, device_id={"lev": peer}, device_id_type=MESH)
 
-    def greet(peer):
-        pl.semaphore_signal(barrier, inc=1, device_id={"horiz": peer}, device_id_type=MESH)
-
-    for_peers(me, tiles, greet)
+    def greet(semaphore, peer):
+        pl.semaphore_signal(semaphore, inc=1, device_id={"horiz": peer}, device_id_type=MESH)
+
+    plane = RING * CORES
+    line_peers = [lax.rem(me + k * plane, tiles) for k in range(1, RING)]
+    plane_peers = [me // plane * plane + lax.rem(me + k, plane) for k in range(1, plane)]
+    for peer in line_peers + plane_peers:
+        greet(barrier, peer)
 
     def column(row):
         return jnp.broadcast_to(row[...].astype(f32), (obs, obs)).T[:, 0:1]
@@ -185,8 +202,10 @@
     def gather_bands(use):
         return band_copies(tbuf, use, t_send, t_recv, 0, pl.ds(0, HALF))
 
-    pl.semaphore_wait(barrier, tiles - 1 + bands - 1)
+    pl.semaphore_wait(barrier, bands - 1 + len(line_peers) + len(plane_peers))
     copies = gather_bands(0)
+    for peer in plane_peers:
+        greet(entered, peer)
 
     onehot = (column(tile_row) == iota((obs, tiles), 1).astype(f32)).astype(f32)
     same = nt(onehot.astype(bf16), onehot.astype(bf16))
@@ -246,7 +265,7 @@
                 device_id_type=MESH,
             ).start()
 
-        for_peers(me, tiles, send)
+        for_peers(me, send)
         rbuf[use, me] = sbuf[use, me]
 
     def arrived(use):
@@ -330,6 +349,7 @@
     column_slots = nn(sends[...], high) + nn(sends[...], low)
     wait_all(copies)
     put(0, columns(0, 0) + column_slots)
+    pl.semaphore_wait(entered, len(plane_peers))
     exchange(0)
     put(4, columns(0, 1))
     arrived(0)
@@ -399,6 +419,11 @@
     ).reshape(shape)
     for use in range(7):
         left(use)
+
+
+def hand_on(a_in, b_in, a_out, b_out):
+    a_out[...] = a_in[...]
+    b_out[...] = b_in[...]
 
 
 def shards(
@@ -446,6 +471,7 @@
             pltpu.VMEM((3, obs, channels), f32),
             pltpu.VMEM((2, obs, channels), f32),
             pltpu.VMEM((2, variables * band, COLS), f32),
+            pltpu.SemaphoreType.REGULAR,
             dma((7,)),
             dma((3, 1, bands)),
             dma((3, 1, bands)),
@@ -467,7 +493,14 @@
         precision_off,
         vertical_factor,
     )
-    return increment, residual
+    return pl.pallas_call(
+        hand_on,
+        out_shape=(out, out),
+        in_specs=[vmem] * 2,
+        out_specs=[vmem] * 2,
+        compiler_params=pltpu.CompilerParams(vmem_limit_bytes=60 << 20),
+        name="outputs",
+    )(increment, residual)
 
 
 def solution(mesh):

time: 86.6 us -> 83 us (0.958)
  local copies, waits for them, and re-layouts: 3.15 us -> 0 us
    unnamed x2 -> x0, local copies, waits for them, and re-layouts: 3.15 us -> none
    pallas_call x1, Pallas kernels: 82.6 us -> 80.5 us  [shards(): pl.pallas_call(functools.partial(kernel, tiles, bands), out_shape=(out, o...]
    pallas_call x0 -> x1, Pallas kernels: none -> 1.69 us  [shards(): pl.pallas_call(hand_on, out_shape=(out, out), in_specs=[vmem] * 2, out_sp...]
where the time goes in v4:
time: 83 us; the launch traced here: 82.8 us
  Pallas kernels  82.2 us (99%)
    pallas_call x1, Pallas kernels, shards(): pl.pallas_call(functools.partial(kernel, tiles, bands), out_shape=(out, o...  80.5 us
    pallas_call x1, Pallas kernels, shards(): pl.pallas_call(hand_on, out_shape=(out, out), in_specs=[vmem] * 2, out_sp...  1.69 us

profile of v4, /device:TPU:1, one launch (start us, length us, event | category | flops | bytes accessed | tf_op | source)
XLA Modules:
  0.0 82.8 jit_solution(7912985582024035835)
XLA Ops:
  0.6 80.5 %analysis.1 = (f32[34,2,512]{2,1,0:T(2,128)}, f32[34,2,512]{2,1,0:T(2,128)}) custom-call(bf16[64,34,2,200]{3,2,1,0:T(2,128)(2,1)} %bitcast.4, s32[1,64]{1,0:T(1,128)} %bitcast.5, s32[1,64]{1,0:T(1,128)} %bitcast.6, f32[1,64]{1,0:T(1,128)} %bitcast.7, f32[64,200]{1,0:T(8,128)} %innovation_in.1, f32[200,200]{1,0:T(8,128)} %precision_in.1, ...), custom_call_target="tpu_custom_call" | custom-call | tf_op jit(solution)/shard_map/analysis/pallas_call | solution.py:446
  81.1 1.7 %outputs.1 = (f32[34,2,512]{2,1,0:T(2,128)}, f32[34,2,512]{2,1,0:T(2,128)}) custom-call(f32[34,2,512]{2,1,0:T(2,128)} %get-tuple-element.4.a_in, f32[34,2,512]{2,1,0:T(2,128)} %get-tuple-element.5.b_in), custom_call_target="tpu_custom_call" | custom-call | tf_op jit(solution)/shard_map/outputs/pallas_call | solution.py:496

commit v5 on v4

--- a/solution.py
+++ b/solution.py
@@ -81,7 +81,8 @@
     precision_off,
     vertical,
     jpad,
-    rmat,
+    rmat_high,
+    rmat_low,
     coef_high,
     coef_low,
     picks,
@@ -90,6 +91,7 @@
     repeat,
     tbuf,
     ibuf,
+    own_images,
     sbuf,
     rbuf,
     w_buf,
@@ -150,20 +152,19 @@
     weight = column(weight_row)
     off = precision_off[...]
     eye_c = (iota((channels, channels), 0) == iota((channels, channels), 1)).astype(f32)
-    rmat[...] = eye_c + 0.5 * (off + off.T)
-
-    w0 = (weight * nn(innovation[...], rmat[...], HIGHEST)).astype(bf16)
+    rmat = eye_c + 0.5 * (off + off.T)
+    rmat_high[...], rmat_low[...] = split(rmat)
+
+    w0 = (weight * nn(innovation[...], rmat, HIGHEST)).astype(bf16)
     w_buf[0] = w0.astype(f32)
 
-    fetches[5].wait()
-
-    @pl.loop(0, obs, unroll=4)
-    def _(o):
-        start = pl.multiple_of(o * SLAB, 16)
-        jpad[pl.ds(start + 64, 16), :] = jnp.zeros((16, channels), bf16)
-        jpad[pl.ds(start, used), :] = jraw[o].reshape(used, channels)
-
-    def adjoint(high, low, part, parts, total):
+    def fill(g):
+        for o in range(g * GROUP, (g + 1) * GROUP):
+            start = o * SLAB
+            jpad[start + 64 : start + SLAB, :] = jnp.zeros((SLAB - 64, channels), bf16)
+            jpad[start : start + used, :] = jraw[o].reshape(used, channels)
+
+    def adjoint(high, low, part, parts, total, ready=lambda g: None):
         groups = obs // GROUP // parts
         rows = groups * GROUP
         before = [jnp.zeros((rows, channels), bf16)] * part
@@ -171,6 +172,7 @@
         both = jnp.concatenate([*before, high, *after, *before, low, *after], axis=0)
         lane = lax.rem(iota((SLAB, 2 * obs), 1), obs)
         for g in range(part * groups, (part + 1) * groups):
+            ready(g)
             product = nt(jpad[g * GROUP * SLAB : (g + 1) * GROUP * SLAB, :], both)
             for j in range(GROUP):
                 mine = lane == g * GROUP + j
@@ -182,7 +184,8 @@
         tbuf[use, lev] = jnp.where(iota((HALF, 2 * obs), 1) < obs, t[0:HALF, :], t[HALF:, :])
 
     no_terms = jnp.zeros((SLAB, 2 * obs), f32)
-    store_terms(0, adjoint(w0, jnp.zeros_like(w0), 0, 1, no_terms))
+    fetches[5].wait()
+    store_terms(0, adjoint(w0, jnp.zeros_like(w0), 0, 1, no_terms, fill))
 
     def band_copies(buf, use, send_sem, recv_sem, part, rows):
         copies = []
@@ -316,10 +319,11 @@
                 [spread[at : at + GROUP, :], spread[obs + at : obs + at + GROUP, :]], axis=0
             )
             part = nn(lhs.astype(bf16), jpad[at * SLAB : (at + GROUP) * SLAB, :])
-            ibuf[use, lev, at : at + GROUP, :] = part[0:GROUP, :] + part[GROUP:, :]
+            own_images[at : at + GROUP, :] = part[0:GROUP, :] + part[GROUP:, :]
             if (g + 1) % groups == 0:
                 p = g // groups
                 rows = pl.ds(p * groups * GROUP, groups * GROUP)
+                ibuf[use, lev, rows, :] = own_images[rows, :].astype(bf16)
                 copies.append(band_copies(ibuf, use, i_send, i_recv, p, rows))
         return copies
 
@@ -329,11 +333,14 @@
         for p in range(parts):
             wait_all(copies[p])
             rows = slice(p * size, (p + 1) * size)
-            total = ibuf[use, 0, rows, :]
-            for m in range(1, bands):
-                total = total + ibuf[use, m, rows, :]
+            total = own_images[rows, :]
+            for k in range(1, bands):
+                total = total + ibuf[use, lax.rem(lev + k, bands), rows, :].astype(f32)
             im_buf[use, rows, :] = total
-            w = weight[rows, :] * nn(total, rmat[...], HIGHEST)
+            high, low = split(total)
+            both = nn(jnp.concatenate([high, low], axis=0), rmat_high[...])
+            w = both[0:size, :] + (both[size:, :] + nn(high, rmat_low[...]))
+            w = weight[rows, :] * w
             w_buf[use + 1, rows, :] = w
             high, low = split(w)
             terms = adjoint(high, low, p, parts, terms)
@@ -457,7 +464,8 @@
             pltpu.VMEM((channels, channels), f32),
             pltpu.VMEM(vertical_factor.shape, f32),
             pltpu.VMEM((obs * SLAB, channels), bf16),
-            pltpu.VMEM((channels, channels), f32),
+            pltpu.VMEM((channels, channels), bf16),
+            pltpu.VMEM((channels, channels), bf16),
             pltpu.VMEM((2 * LANES, 2 * bands * HALF), bf16),
             pltpu.VMEM((2 * LANES, 2 * bands * HALF), bf16),
             pltpu.VMEM((obs, 2 * tiles), bf16),
@@ -465,7 +473,8 @@
             pltpu.VMEM((2 * tiles, 2 * tiles), bf16),
             pltpu.VMEM((LANES, GROUP * SLAB), bf16),
             pltpu.VMEM((3, bands, HALF, 2 * obs), f32),
-            pltpu.VMEM((2, bands, obs, channels), f32),
+            pltpu.VMEM((2, bands, obs, channels), bf16),
+            pltpu.VMEM((obs, channels), f32),
             pltpu.VMEM((7, tiles, 2, LANES), f32),
             pltpu.VMEM((7, tiles, 2, LANES), f32),
             pltpu.VMEM((3, obs, channels), f32),

time: 83 us -> 80.5 us (0.970)
  Pallas kernels: 82.2 us -> 79.7 us
    pallas_call x1, Pallas kernels: 80.5 us -> 78 us  [shards(): pl.pallas_call(functools.partial(kernel, tiles, bands), out_shape=(out, o...]
where the time goes in v5:
time: 80.5 us; the launch traced here: 80.3 us
  Pallas kernels  79.7 us (99%)
    pallas_call x1, Pallas kernels, shards(): pl.pallas_call(functools.partial(kernel, tiles, bands), out_shape=(out, o...  78 us
    pallas_call x1, Pallas kernels, shards(): pl.pallas_call(hand_on, out_shape=(out, out), in_specs=[vmem] * 2, out_sp...  1.69 us

profile of v5, /device:TPU:1, one launch (start us, length us, event | category | flops | bytes accessed | tf_op | source)
XLA Modules:
  0.0 80.3 jit_solution(16946991158076403615)
XLA Ops:
  0.6 78.0 %analysis.1 = (f32[34,2,512]{2,1,0:T(2,128)}, f32[34,2,512]{2,1,0:T(2,128)}) custom-call(bf16[64,34,2,200]{3,2,1,0:T(2,128)(2,1)} %bitcast.4, s32[1,64]{1,0:T(1,128)} %bitcast.5, s32[1,64]{1,0:T(1,128)} %bitcast.6, f32[1,64]{1,0:T(1,128)} %bitcast.7, f32[64,200]{1,0:T(8,128)} %innovation_in.1, f32[200,200]{1,0:T(8,128)} %precision_in.1, ...), custom_call_target="tpu_custom_call" | custom-call | tf_op jit(solution)/shard_map/analysis/pallas_call | solution.py:453
  78.7 1.7 %outputs.1 = (f32[34,2,512]{2,1,0:T(2,128)}, f32[34,2,512]{2,1,0:T(2,128)}) custom-call(f32[34,2,512]{2,1,0:T(2,128)} %get-tuple-element.4.a_in, f32[34,2,512]{2,1,0:T(2,128)} %get-tuple-element.5.b_in), custom_call_target="tpu_custom_call" | custom-call | tf_op jit(solution)/shard_map/outputs/pallas_call | solution.py:505

commit v6 on v5

--- a/solution.py
+++ b/solution.py
@@ -14,6 +14,7 @@
 SLAB = 80
 HALF = SLAB // 2
 GROUP = 8
+CHUNKS = 2
 RING = 8
 CORES = 2
 COL_LANE = 127
@@ -114,6 +115,8 @@
     used = 2 * band
     f32, bf16 = jnp.float32, jnp.bfloat16
 
+    chunk = obs // CHUNKS
+    chunks = [pl.ds(c * chunk, chunk) for c in range(CHUNKS)]
     fetches = [
         pltpu.make_async_copy(source, target, in_sem.at[at])
         for at, (source, target) in enumerate(
@@ -123,7 +126,7 @@
                 (weight_in, weight_row),
                 (tile_in, tile_row),
                 (column_in, column_row),
-                (jac, jraw),
+                *((jac.at[rows], jraw.at[rows]) for rows in chunks),
                 (vertical_in, vertical),
             )
         )
@@ -159,6 +162,8 @@
     w_buf[0] = w0.astype(f32)
 
     def fill(g):
+        if g * GROUP % chunk == 0:
+            fetches[5 + g * GROUP // chunk].wait()
         for o in range(g * GROUP, (g + 1) * GROUP):
             start = o * SLAB
             jpad[start + 64 : start + SLAB, :] = jnp.zeros((SLAB - 64, channels), bf16)
@@ -184,8 +189,9 @@
         tbuf[use, lev] = jnp.where(iota((HALF, 2 * obs), 1) < obs, t[0:HALF, :], t[HALF:, :])
 
     no_terms = jnp.zeros((SLAB, 2 * obs), f32)
-    fetches[5].wait()
     store_terms(0, adjoint(w0, jnp.zeros_like(w0), 0, 1, no_terms, fill))
+
+    under_way = []
 
     def band_copies(buf, use, send_sem, recv_sem, part, rows):
         copies = []
@@ -200,6 +206,7 @@
             )
             copy.start()
             copies.append(copy)
+        under_way.extend(copies)
         return copies
 
     def gather_bands(use):
@@ -225,7 +232,7 @@
         iota((LANES, GROUP * SLAB), 0) == lax.rem(iota((LANES, GROUP * SLAB), 1), SLAB)
     ).astype(bf16)
 
-    fetches[6].wait()
+    fetches[-1].wait()
 
     row = iota((LANES, levels), 0)
     wide = iota((levels, 2 * bands * HALF), 1)
@@ -249,9 +256,8 @@
         gathered = jnp.concatenate([gathered, pltpu.roll(gathered, obs, 1)], axis=0)
         high, low = split(gathered)
         rows = pl.ds(part * LANES, LANES)
-        mapped = nn(coef_high[rows, :], high) + (
-            nn(coef_high[rows, :], low) + nn(coef_low[rows, :], high)
-        )
+        mapped = nn(coef_high[rows, :], jnp.concatenate([high, low], axis=1))
+        mapped = mapped[:, 0 : 2 * obs] + (mapped[:, 2 * obs :] + nn(coef_low[rows, :], high))
         mapped = jnp.where(iota((LANES, 2 * obs), 1) < obs, mapped, 0.0)
         high, low = split(mapped)
         slots = nt(sends[...], jnp.concatenate([high, low], axis=0))
@@ -348,7 +354,7 @@
 
     def wait_all(copies):
         for copy in copies:
-            copy.wait()
+            copy.wait_recv()
 
     column_rhs = jnp.concatenate([column(column_row) + 1.0, jnp.zeros((obs, 1), f32)], axis=0)
     column_rhs = jnp.where(iota((2 * obs, LANES), 1) == COL_LANE, column_rhs, 0.0)
@@ -424,6 +430,8 @@
     residual[...] = (
         (keep - a1 * k0) * v0 - (a0 + a1 * mixed) * v1 - a1 * k1 * v2
     ).reshape(shape)
+    for copy in under_way:
+        copy.wait_send()
     for use in range(7):
         left(use)
 
@@ -481,7 +489,7 @@
             pltpu.VMEM((2, obs, channels), f32),
             pltpu.VMEM((2, variables * band, COLS), f32),
             pltpu.SemaphoreType.REGULAR,
-            dma((7,)),
+            dma((6 + CHUNKS,)),
             dma((3, 1, bands)),
             dma((3, 1, bands)),
             dma((2, 2, bands)),

time: 80.5 us -> 80.1 us (level)
  no operation moved by 1% of the time
where the time goes in v6:
time: 80.1 us; the launch traced here: 79.9 us
  Pallas kernels  79.3 us (99%)
    pallas_call x1, Pallas kernels, shards(): pl.pallas_call(functools.partial(kernel, tiles, bands), out_shape=(out, o...  77.6 us
    pallas_call x1, Pallas kernels, shards(): pl.pallas_call(hand_on, out_shape=(out, out), in_specs=[vmem] * 2, out_sp...  1.69 us

profile of v6, /device:TPU:1, one launch (start us, length us, event | category | flops | bytes accessed | tf_op | source)
XLA Modules:
  0.0 79.9 jit_solution(14719788008885308046)
XLA Ops:
  0.6 77.6 %analysis.1 = (f32[34,2,512]{2,1,0:T(2,128)}, f32[34,2,512]{2,1,0:T(2,128)}) custom-call(bf16[64,34,2,200]{3,2,1,0:T(2,128)(2,1)} %bitcast.4, s32[1,64]{1,0:T(1,128)} %bitcast.5, s32[1,64]{1,0:T(1,128)} %bitcast.6, f32[1,64]{1,0:T(1,128)} %bitcast.7, f32[64,200]{1,0:T(8,128)} %innovation_in.1, f32[200,200]{1,0:T(8,128)} %precision_in.1, ...), custom_call_target="tpu_custom_call" | custom-call | tf_op jit(solution)/shard_map/analysis/pallas_call | solution.py:461
  78.3 1.7 %outputs.1 = (f32[34,2,512]{2,1,0:T(2,128)}, f32[34,2,512]{2,1,0:T(2,128)}) custom-call(f32[34,2,512]{2,1,0:T(2,128)} %get-tuple-element.4.a_in, f32[34,2,512]{2,1,0:T(2,128)} %get-tuple-element.5.b_in), custom_call_target="tpu_custom_call" | custom-call | tf_op jit(solution)/shard_map/outputs/pallas_call | solution.py:513
